TPU v7x, 32 devices: a whole 2x2x4 slice. The times are simulated.
32 devices in a mesh: rows: 4 (over y, core), cols: 8 (over z, x).
Axes of the slice: x: 2, y: 2, z: 4, core: 2. Of those that a mesh axis runs over, the one named last changes fastest.
Arguments:
- tokens: bfloat16 [2048, 2048], P('rows', 'cols'), may hold values from -6 to 6
- cotangent: bfloat16 [2048, 2048], P('rows', 'cols'), may hold values from -6 to 6
- lengths: int32 [4, 3], P('rows'), may hold values from 1 to 256, 512 in all within a row
- decay_rate: float32 [16], P('cols'), may hold values from 0.003 to 0.06
- query_weight: bfloat16 [2048, 2048], P('rows', 'cols'), may hold values from -0.125 to 0.125
- key_weight: bfloat16 [2048, 2048], P('rows', 'cols'), may hold values from -0.125 to 0.125
- value_weight: bfloat16 [2048, 2048], P('rows', 'cols'), may hold values from -0.125 to 0.125
- gate_weight: bfloat16 [2048, 2048], P('rows', 'cols'), may hold values from -0.125 to 0.125
- out_weight: bfloat16 [2048, 2048], P('cols', 'rows'), may hold values from -0.25 to 0.25
- first_weight: bfloat16 [2048, 5632], P('rows', 'cols'), may hold values from -0.125 to 0.125
- second_weight: bfloat16 [2048, 5632], P('rows', 'cols'), may hold values from -0.125 to 0.125
- down_weight: bfloat16 [5632, 2048], P('cols', 'rows'), may hold values from -0.078125 to 0.078125
Outputs:
- layer_out: bfloat16 [2048, 2048], P('rows', 'cols')
- token_grad: float32 [2048, 2048], P('rows', 'cols')
- query_grad: float32 [2048, 2048], P('rows', 'cols')
- key_grad: float32 [2048, 2048], P('rows', 'cols')
- value_grad: float32 [2048, 2048], P('rows', 'cols')
- gate_grad: float32 [2048, 2048], P('rows', 'cols')
- out_grad: float32 [2048, 2048], P('cols', 'rows')
- first_grad: float32 [2048, 5632], P('rows', 'cols')
- second_grad: float32 [2048, 5632], P('rows', 'cols')
- down_grad: float32 [5632, 2048], P('cols', 'rows')
Inputs may be any that keep to these rules, and one draw needn't show every extreme that they name: Each group's lengths add up to 512, and in every group the longest is exactly 256.
All inputs are finite; a program needn't handle non-finite values.
Results may differ from a plain program's by a relative error of at most 0.014.
Values may be sent and summed in bfloat16 or wider, within the bound.
No kernel may reach another device: no remote copies, remote signals or barrier semaphores. Data moves between devices by JAX's collectives and lax.ppermute only.
A program may use at most 192 MiB of HBM per device.

v0:
```python
import jax
import jax.numpy as jnp
from jax import lax
from jax.sharding import PartitionSpec as P

HEAD = 128
LEN_CAP = 1024


EPSILON = 1e-06


def rms_scaled(values):
    inverse_rms = lax.rsqrt(jnp.mean(values * values, axis=-1, keepdims=True) + EPSILON)
    return (values * inverse_rms, inverse_rms)


def contract_rows(left_side, right_side):
    return lax.dot_general(
        left_side, right_side, (((0,), (0,)), ((), ())), preferred_element_type=jnp.float32
    )


def contract_cols(left_side, right_side):
    return lax.dot_general(
        left_side, right_side, (((1,), (1,)), ((), ())), preferred_element_type=jnp.float32
    )


def silu_slope(values):
    sigmoid_of = jax.nn.sigmoid(values)
    return sigmoid_of * (1.0 + values * (1.0 - sigmoid_of))


def decay_block(first_row, block_rows, key_start, key_rows, member, decay_rates):
    key_places = key_start + jnp.arange(key_rows, dtype=jnp.int32)
    rows_here = first_row + jnp.arange(block_rows, dtype=jnp.int32)
    distance = (rows_here[:, None] - key_places[None, :]).astype(jnp.float32)
    allowed = (member[:, None] == member[None, :]) & (distance >= 0)
    return jnp.where(
        allowed[None], jnp.exp(-decay_rates[:, None, None] * jnp.maximum(distance, 0.0)[None]), 0.0
    )


def shards(
    tokens,
    cotangent,
    lengths,
    decay_rate,
    query_weight,
    key_weight,
    value_weight,
    gate_weight,
    out_weight,
    first_weight,
    second_weight,
    down_weight,
):
    gathered, grad_rows = (
        lax.all_gather(tokens, "cols", axis=1, tiled=True),
        lax.all_gather(cotangent, "cols", axis=1, tiled=True),
    )
    full_weights = (
        lax.all_gather(query_weight, "rows", axis=0, tiled=True),
        lax.all_gather(key_weight, "rows", axis=0, tiled=True),
        lax.all_gather(value_weight, "rows", axis=0, tiled=True),
        lax.all_gather(gate_weight, "rows", axis=0, tiled=True),
        lax.all_gather(out_weight, "rows", axis=1, tiled=True),
        lax.all_gather(first_weight, "rows", axis=0, tiled=True),
        lax.all_gather(second_weight, "rows", axis=0, tiled=True),
        lax.all_gather(down_weight, "rows", axis=1, tiled=True),
    )
    query_full, key_full, value_full, gate_full, out_full, first_full, second_full, down_full = (
        full_weights
    )
    token_count, model_width = gathered.shape
    local_width = tokens.shape[1]
    head_width = query_full.shape[1]
    local_heads = head_width // HEAD
    hidden_local = first_full.shape[1]
    column_start = lax.axis_index("cols") * local_width

    def to_heads(array):
        return array.reshape(token_count, local_heads, HEAD)

    inputs_full = gathered.astype(jnp.float32)
    normed, inverse_first = rms_scaled(inputs_full)
    normed_low = normed.astype(jnp.bfloat16)
    proj_weights = jnp.concatenate((query_full, key_full, value_full, gate_full), axis=1)
    projected = jnp.dot(normed_low, proj_weights, preferred_element_type=jnp.float32)
    pre_query = projected[:, :head_width]
    pre_key = projected[:, head_width : 2 * head_width]
    pre_value = projected[:, 2 * head_width : 3 * head_width]
    pre_gate = projected[:, 3 * head_width :]
    queries = to_heads(jax.nn.silu(pre_query).astype(jnp.bfloat16))
    keys = to_heads(jax.nn.silu(pre_key).astype(jnp.bfloat16))
    values = to_heads(jax.nn.silu(pre_value).astype(jnp.bfloat16))
    bounds = jnp.cumsum(lengths[0])
    places = jnp.arange(token_count, dtype=jnp.int32)
    member = jnp.sum((places[:, None] >= bounds[None, :]).astype(jnp.int32), axis=1)
    block_rows = min(512, token_count)
    window = min(token_count, block_rows + min(LEN_CAP, token_count // 2))
    block_starts = jnp.arange(token_count // block_rows, dtype=jnp.int32) * block_rows

    def window_start(first_row):
        return jnp.maximum(first_row + block_rows - window, 0)

    def attend(first_row):
        key_start = window_start(first_row)
        weights = decay_block(first_row, block_rows, key_start, window, member, decay_rate)
        scores = jnp.einsum("qhd,khd->hqk", queries, keys, preferred_element_type=jnp.float32)
        score_mix = (scores * weights).astype(jnp.bfloat16)
        return jnp.einsum("hqk,khd->qhd", score_mix, values, preferred_element_type=jnp.float32)

    attended = lax.map(attend, block_starts).reshape(token_count, head_width)
    square_sums = lax.psum(jnp.sum(attended * attended, axis=1), "cols")
    inverse_attn = lax.rsqrt(square_sums / model_width + EPSILON)[:, None]
    attn_normed = attended * inverse_attn
    gate_value = jax.nn.sigmoid(pre_gate)
    gated_low = (attn_normed * gate_value).astype(jnp.bfloat16)
    partial_attn = jnp.dot(gated_low, out_full, preferred_element_type=jnp.float32)
    branch = lax.psum_scatter(partial_attn, "cols", scatter_dimension=1, tiled=True)
    middle = tokens.astype(jnp.float32) + branch
    middle_low = lax.all_gather(middle.astype(jnp.bfloat16), "cols", axis=1, tiled=True)
    normed_two, inverse_second = rms_scaled(middle_low.astype(jnp.float32))
    normed_two_low = normed_two.astype(jnp.bfloat16)
    pair_weights = jnp.concatenate((first_full, second_full), axis=1)
    pair = jnp.dot(normed_two_low, pair_weights, preferred_element_type=jnp.float32)
    first_act = pair[:, :hidden_local]
    second_act = pair[:, hidden_local:]
    hidden_low = (first_act * second_act).astype(jnp.bfloat16)
    ffn_out = lax.psum_scatter(
        jnp.dot(hidden_low, down_full, preferred_element_type=jnp.float32),
        "cols",
        scatter_dimension=1,
        tiled=True,
    )
    layer_out = (middle + ffn_out).astype(jnp.bfloat16)
    hidden_grad = contract_cols(grad_rows, down_full)
    down_grad = contract_rows(hidden_low, grad_rows)
    first_low = (hidden_grad * second_act).astype(jnp.bfloat16)
    second_low = (hidden_grad * first_act).astype(jnp.bfloat16)
    pair_grad = jnp.concatenate((first_low, second_low), axis=1)
    pair_weight_grad = contract_rows(normed_two_low, pair_grad)
    normed_two_grad = lax.psum_scatter(
        contract_cols(pair_grad, pair_weights), "cols", scatter_dimension=1, tiled=True
    )
    normed_two_here = lax.dynamic_slice_in_dim(normed_two, column_start, local_width, 1)
    second_stat = lax.psum(jnp.sum(normed_two_grad * normed_two_here, axis=1), "cols")
    middle_grad = cotangent.astype(jnp.float32) + inverse_second * (
        normed_two_grad - normed_two_here * (second_stat / model_width)[:, None]
    )
    branch_rows = lax.all_gather(middle_grad.astype(jnp.bfloat16), "cols", axis=1, tiled=True)
    gated_grad = contract_cols(branch_rows, out_full)
    out_grad = contract_rows(gated_low, branch_rows)
    normed_attn_grad = gated_grad * gate_value
    pre_gate_grad = gated_grad * attn_normed * gate_value * (1.0 - gate_value)
    first_stat = lax.psum(jnp.sum(normed_attn_grad * attn_normed, axis=1), "cols")
    attended_grad = inverse_attn * (
        normed_attn_grad - attn_normed * (first_stat / model_width)[:, None]
    )
    attended_low = to_heads(attended_grad.astype(jnp.bfloat16))

    def attend_back(carry, first_row):
        key_sum, value_sum = carry
        key_start = window_start(first_row)
        weights = decay_block(first_row, block_rows, key_start, window, member, decay_rate)
        scores = jnp.einsum("qhd,khd->hqk", queries, keys, preferred_element_type=jnp.float32)
        score_mix = (scores * weights).astype(jnp.bfloat16)
        score_grad = jnp.einsum(
            "qhd,khd->hqk", attended_low, values, preferred_element_type=jnp.float32
        )
        raw_grad = (score_grad * weights).astype(jnp.bfloat16)
        query_part = jnp.einsum("hqk,khd->qhd", raw_grad, keys, preferred_element_type=jnp.float32)
        key_part = jnp.einsum("hqk,qhd->khd", raw_grad, queries, preferred_element_type=jnp.float32)
        value_part = jnp.einsum(
            "hqk,qhd->khd", score_mix, attended_low, preferred_element_type=jnp.float32
        )
        key_sum = key_sum + key_part
        value_sum = value_sum + value_part
        return ((key_sum, value_sum), query_part)

    zero_heads = jnp.zeros((token_count, local_heads, HEAD), jnp.float32)
    (key_total, value_total), query_parts = lax.scan(
        attend_back, (zero_heads, zero_heads), block_starts
    )
    query_total = query_parts.reshape(token_count, head_width)
    key_flat = key_total.reshape(token_count, head_width)
    value_flat = value_total.reshape(token_count, head_width)
    proj_grad = jnp.concatenate(
        (
            (query_total * silu_slope(pre_query)).astype(jnp.bfloat16),
            (key_flat * silu_slope(pre_key)).astype(jnp.bfloat16),
            (value_flat * silu_slope(pre_value)).astype(jnp.bfloat16),
            pre_gate_grad.astype(jnp.bfloat16),
        ),
        axis=1,
    )
    proj_weight_grad = contract_rows(normed_low, proj_grad)
    normed_grad = lax.psum_scatter(
        contract_cols(proj_grad, proj_weights), "cols", scatter_dimension=1, tiled=True
    )
    normed_here = lax.dynamic_slice_in_dim(normed, column_start, local_width, 1)
    zero_stat = lax.psum(jnp.sum(normed_grad * normed_here, axis=1), "cols")
    token_grad = middle_grad + inverse_first * (
        normed_grad - normed_here * (zero_stat / model_width)[:, None]
    )
    summed = (
        lax.psum_scatter(proj_weight_grad[:, :head_width], "rows", scatter_dimension=0, tiled=True),
        lax.psum_scatter(
            proj_weight_grad[:, head_width : 2 * head_width],
            "rows",
            scatter_dimension=0,
            tiled=True,
        ),
        lax.psum_scatter(
            proj_weight_grad[:, 2 * head_width : 3 * head_width],
            "rows",
            scatter_dimension=0,
            tiled=True,
        ),
        lax.psum_scatter(
            proj_weight_grad[:, 3 * head_width :], "rows", scatter_dimension=0, tiled=True
        ),
        lax.psum_scatter(out_grad, "rows", scatter_dimension=1, tiled=True),
        lax.psum_scatter(
            pair_weight_grad[:, :hidden_local], "rows", scatter_dimension=0, tiled=True
        ),
        lax.psum_scatter(
            pair_weight_grad[:, hidden_local:], "rows", scatter_dimension=0, tiled=True
        ),
        lax.psum_scatter(down_grad, "rows", scatter_dimension=1, tiled=True),
    )
    return (
        layer_out,
        token_grad,
        summed[0],
        summed[1],
        summed[2],
        summed[3],
        summed[4],
        summed[5],
        summed[6],
        summed[7],
    )


def solution(mesh):
    placed = (
        P("rows", "cols"),
        P("rows", "cols"),
        P("rows", None),
        P("cols"),
        P("rows", "cols"),
        P("rows", "cols"),
        P("rows", "cols"),
        P("rows", "cols"),
        P("cols", "rows"),
        P("rows", "cols"),
        P("rows", "cols"),
        P("cols", "rows"),
    )
    return jax.shard_map(
        shards,
        mesh=mesh,
        in_specs=placed,
        out_specs=(
            P("rows", "cols"),
            P("rows", "cols"),
            P("rows", "cols"),
            P("rows", "cols"),
            P("rows", "cols"),
            P("rows", "cols"),
            P("cols", "rows"),
            P("rows", "cols"),
            P("rows", "cols"),
            P("cols", "rows"),
        ),
        check_vma=False,
    )
```

profile of v0, /device:TPU:0, one launch (start us, length us, event | category | flops | bytes accessed | tf_op | source)
XLA Modules:
  0.0 1159.7 jit_solution(5291965990124624452)
XLA Ops:
  12.9 16.1 %all-gather.15.cloned.1.call-done = bf16[2048,256]{1,0:T(8,128)(2,1)} async-done(((bf16[512,256]{1,0:T(8,128)(2,1)}), bf16[2048,256]{1,0:T(8,128)(2,1)}) %all-gather.15.cloned.1.call-update) | async-done | bytes 1048592 | tf_op jit(solution)/shard_map/all_gather | solution.py:64
  31.4 15.9 %all-gather.17.cloned.1.call-done = bf16[2048,256]{1,0:T(8,128)(2,1)} async-done(((bf16[512,256]{1,0:T(8,128)(2,1)}), bf16[2048,256]{1,0:T(8,128)(2,1)}) %all-gather.17.cloned.1.call-update) | async-done | bytes 1048592 | tf_op jit(solution)/shard_map/all_gather | solution.py:65
  49.7 16.0 %all-gather.19.cloned.1.call-done = bf16[2048,256]{1,0:T(8,128)(2,1)} async-done(((bf16[512,256]{1,0:T(8,128)(2,1)}), bf16[2048,256]{1,0:T(8,128)(2,1)}) %all-gather.19.cloned.1.call-update) | async-done | bytes 1048592 | tf_op jit(solution)/shard_map/all_gather | solution.py:66
  68.0 15.8 %all-gather.21.cloned.1.call-done = bf16[2048,256]{1,0:T(8,128)(2,1)} async-done(((bf16[512,256]{1,0:T(8,128)(2,1)}), bf16[2048,256]{1,0:T(8,128)(2,1)}) %all-gather.21.cloned.1.call-update) | async-done | bytes 1048592 | tf_op jit(solution)/shard_map/all_gather | solution.py:67
  86.2 50.7 %all-gather.13.cloned.1.call-done = bf16[512,2048]{1,0:T(8,128)(2,1)} async-done(((bf16[512,256]{1,0:T(8,128)(2,1)}), bf16[512,2048]{1,0:T(8,128)(2,1)}) %all-gather.13.cloned.1.call-update) | async-done | bytes 2097168 | tf_op jit(solution)/shard_map/all_gather | solution.py:60
  149.0 18.6 %psum.28 = f32[512]{0:T(512)S(1)} all-reduce(f32[512]{0:T(512)S(1)} %get-tuple-element.78), channel_id=1, replica_groups=mesh['rows'=4,'cols'=8] {'cols'}, use_global_device_ids=true, to_apply=%region_4.5 | all-reduce | flops 512 | bytes 4096 | tf_op jit(solution)/shard_map/psum | solution.py:116
  174.3 84.3 %reduce-scatter.13.cloned.1.call-done = f32[512,256]{1,0:T(8,128)} async-done(((f32[512,2048]{1,0:T(8,128)}), f32[512,256]{1,0:T(8,128)}) %reduce-scatter.13.cloned.1.call-update) | async-done | bytes 524304 | tf_op jit(solution)/shard_map/reduce_scatter | solution.py:122
  262.1 25.1 %all-gather.27.cloned.1.call-done = bf16[2048,704]{0,1:T(8,128)(2,1)} async-done(((bf16[512,704]{0,1:T(8,128)(2,1)}), bf16[2048,704]{0,1:T(8,128)(2,1)}) %all-gather.27.cloned.1.call-update) | async-done | bytes 2883600 | tf_op jit(solution)/shard_map/all_gather | solution.py:69
  290.9 25.0 %all-gather.29.cloned.1.call-done = bf16[2048,704]{0,1:T(8,128)(2,1)} async-done(((bf16[512,704]{0,1:T(8,128)(2,1)}), bf16[2048,704]{0,1:T(8,128)(2,1)}) %all-gather.29.cloned.1.call-update) | async-done | bytes 2883600 | tf_op jit(solution)/shard_map/all_gather | solution.py:70
  319.7 50.0 %all-gather.25.cloned.1.call-done = bf16[512,2048]{1,0:T(8,128)(2,1)} async-done(((bf16[512,256]{1,0:T(8,128)(2,1)}), bf16[512,2048]{1,0:T(8,128)(2,1)}) %all-gather.25.cloned.1.call-update) | async-done | bytes 2097168 | tf_op jit(solution)/shard_map/all_gather | solution.py:124
  371.9 7.8 fusion.4
  379.7 41.5 %all-gather.33.cloned.1.call-done = bf16[512,2048]{1,0:T(8,128)(2,1)} async-done(((bf16[512,256]{1,0:T(8,128)(2,1)}), bf16[512,2048]{1,0:T(8,128)(2,1)}) %all-gather.33.cloned.1.call-update) | async-done | bytes 2097168 | tf_op jit(solution)/shard_map/all_gather | solution.py:61
  421.2 26.8 %all-gather.31.cloned.1.call-done = bf16[704,2048]{1,0:T(8,128)(2,1)} async-done(((bf16[704,512]{1,0:T(8,128)(2,1)}), bf16[704,2048]{1,0:T(8,128)(2,1)}) %all-gather.31.cloned.1.call-update) | async-done | bytes 2883600 | tf_op jit(solution)/shard_map/all_gather | solution.py:71
  448.0 6.0 multiply_convert_fusion.3
  455.2 7.7 fusion.11
  467.0 84.5 %reduce-scatter.17.cloned.1.call-done = f32[512,256]{1,0:T(8,128)} async-done(((f32[512,2048]{1,0:T(8,128)}), f32[512,256]{1,0:T(8,128)}) %reduce-scatter.17.cloned.1.call-update) | async-done | bytes 524304 | tf_op jit(solution)/shard_map/reduce_scatter | solution.py:145
  552.9 20.2 %psum.29 = f32[512]{0:T(512)S(1)} all-reduce(f32[512]{0:T(512)S(1)} %multiply_reduce_fusion.2), channel_id=1, replica_groups=mesh['rows'=4,'cols'=8] {'cols'}, use_global_device_ids=true, to_apply=%region_10.11 | all-reduce | flops 512 | bytes 4096 | tf_op jit(solution)/shard_map/psum | solution.py:149
  581.2 42.4 %all-gather.35.cloned.1.call-done = bf16[512,2048]{1,0:T(8,128)(2,1)} async-done(((bf16[512,256]{1,0:T(8,128)(2,1)}), bf16[512,2048]{1,0:T(8,128)(2,1)}) %all-gather.35.cloned.1.call-update) | async-done | bytes 2097168 | tf_op jit(solution)/shard_map/all_gather | solution.py:153
  627.2 19.6 %psum.30 = f32[512]{0:T(512)S(1)} all-reduce(f32[512]{0:T(512)S(1)} %get-tuple-element.80), channel_id=1, replica_groups=mesh['rows'=4,'cols'=8] {'cols'}, use_global_device_ids=true, to_apply=%region_12.13 | all-reduce | flops 512 | bytes 4096 | tf_op jit(solution)/shard_map/psum | solution.py:158
  667.2 6.6 fusion.23
  674.9 9.6 fusion.2
  684.5 10.7 fusion.30
  719.7 86.5 %reduce-scatter.19.cloned.1.call-done = f32[512,256]{1,0:T(8,128)} async-done(((f32[512,2048]{1,0:T(8,128)}), f32[512,256]{1,0:T(8,128)}) %reduce-scatter.19.cloned.1.call-update) | async-done | bytes 524304 | tf_op jit(solution)/shard_map/reduce_scatter | solution.py:200
  807.6 20.2 %psum.31 = f32[512]{0:T(512)S(1)} all-reduce(f32[512]{0:T(512)S(1)} %multiply_reduce_fusion), channel_id=1, replica_groups=mesh['rows'=4,'cols'=8] {'cols'}, use_global_device_ids=true, to_apply=%region_15.16 | all-reduce | flops 512 | bytes 4096 | tf_op jit(solution)/shard_map/psum | solution.py:204
  830.3 33.6 %reduce-scatter.31.cloned.1.call-done = f32[512,704]{0,1:T(8,128)} async-done(((f32[2048,704]{0,1:T(8,128)}), f32[512,704]{0,1:T(8,128)}) %reduce-scatter.31.cloned.1.call-update) | async-done | bytes 1441808 | tf_op jit(solution)/shard_map/reduce_scatter | solution.py:226
  863.8 58.0 %reduce-scatter.33.cloned.1.call-done = f32[512,704]{0,1:T(8,128)} async-done(((f32[2048,704]{0,1:T(8,128)}), f32[512,704]{0,1:T(8,128)}) %reduce-scatter.33.cloned.1.call-update) | async-done | bytes 1441808 | tf_op jit(solution)/shard_map/reduce_scatter | solution.py:229
  921.9 58.0 %reduce-scatter.35.cloned.1.call-done = f32[704,512]{1,0:T(8,128)} async-done(((f32[704,2048]{1,0:T(8,128)}), f32[704,512]{1,0:T(8,128)}) %reduce-scatter.35.cloned.1.call-update) | async-done | bytes 1441808 | tf_op jit(solution)/shard_map/reduce_scatter | solution.py:232
  979.9 34.6 %reduce-scatter.21.cloned.1.call-done = f32[512,256]{1,0:T(8,128)} async-done(((f32[2048,256]{1,0:T(8,128)}), f32[512,256]{1,0:T(8,128)}) %reduce-scatter.21.cloned.1.call-update) | async-done | bytes 524304 | tf_op jit(solution)/shard_map/reduce_scatter | solution.py:209
  1014.5 34.5 %reduce-scatter.23.cloned.1.call-done = f32[512,256]{1,0:T(8,128)} async-done(((f32[2048,256]{1,0:T(8,128)}), f32[512,256]{1,0:T(8,128)}) %reduce-scatter.23.cloned.1.call-update) | async-done | bytes 524304 | tf_op jit(solution)/shard_map/reduce_scatter | solution.py:210
  1049.0 34.8 %reduce-scatter.25.cloned.1.call-done = f32[512,256]{1,0:T(8,128)} async-done(((f32[2048,256]{1,0:T(8,128)}), f32[512,256]{1,0:T(8,128)}) %reduce-scatter.25.cloned.1.call-update) | async-done | bytes 524304 | tf_op jit(solution)/shard_map/reduce_scatter | solution.py:216
  1083.8 34.6 %reduce-scatter.27.cloned.1.call-done = f32[512,256]{1,0:T(8,128)} async-done(((f32[2048,256]{1,0:T(8,128)}), f32[512,256]{1,0:T(8,128)}) %reduce-scatter.27.cloned.1.call-update) | async-done | bytes 524304 | tf_op jit(solution)/shard_map/reduce_scatter | solution.py:222
  1118.3 34.6 %reduce-scatter.29.cloned.1.call-done = f32[256,512]{1,0:T(8,128)} async-done(((f32[256,2048]{1,0:T(8,128)}), f32[256,512]{1,0:T(8,128)}) %reduce-scatter.29.cloned.1.call-update) | async-done | bytes 524304 | tf_op jit(solution)/shard_map/reduce_scatter | solution.py:225
  (160 shorter events, 114.8 us)
Async XLA Ops:
  7.2 5.2 copy-start.24
  7.2 5.2 copy-start.25
  7.2 21.9 %all-gather.15.cloned.1.call-start = ((), (), s32[]{:S(2)}) async-start(), calls=%async_computation.13 | async-start | bytes 1310720 | tf_op jit(solution)/shard_map/all_gather | solution.py:64
  7.9 39.4 %all-gather.17.cloned.1.call-start = ((), (), s32[]{:S(2)}) async-start(), calls=%async_computation.14 | async-start | bytes 1310720 | tf_op jit(solution)/shard_map/all_gather | solution.py:65
  8.7 57.0 %all-gather.19.cloned.1.call-start = ((), (), s32[]{:S(2)}) async-start(), calls=%async_computation.15 | async-start | bytes 1310720 | tf_op jit(solution)/shard_map/all_gather | solution.py:66
  9.4 74.5 %all-gather.21.cloned.1.call-start = ((), (), s32[]{:S(2)}) async-start(), calls=%async_computation.16 | async-start | bytes 1310720 | tf_op jit(solution)/shard_map/all_gather | solution.py:67
  10.0 126.9 %all-gather.13.cloned.1.call-start = ((), (), s32[]{:S(2)}) async-start(), calls=%async_computation.12 | async-start | bytes 2359296 | tf_op jit(solution)/shard_map/all_gather | solution.py:60
  10.6 158.3 %all-gather.23.cloned.1.call-start = ((), (), s32[]{:S(2)}) async-start(), calls=%async_computation.17 | async-start | bytes 1310720 | tf_op jit(solution)/shard_map/all_gather | solution.py:68
  11.2 247.5 %reduce-scatter.13.cloned.1.call-start = ((), (), s32[]{:S(2)}) async-start(), calls=%async_computation.18 | async-start | bytes 4718592 | tf_op jit(solution)/shard_map/reduce_scatter | solution.py:122
  12.9 132.8 %copy-start.15 = (pred[512,512]{1,0:T(8,128)(4,1)}, pred[512,512]{1,0:T(8,128)(4,1)S(1)}, u32[]{:S(2)}) copy-start(pred[512,512]{1,0:T(8,128)(4,1)S(1)} %fusion.10) | copy-start | bytes 786436
  172.8 85.9 %copy-start.7 = (bf16[512,256]{1,0:T(8,128)(2,1)S(1)}, bf16[512,256]{1,0:T(8,128)(2,1)}, u32[]{:S(2)}) copy-start(bf16[512,256]{1,0:T(8,128)(2,1)} %param.12) | copy-start | bytes 786436
  172.8 114.4 %all-gather.27.cloned.1.call-start = ((), (), s32[]{:S(2)}) async-start(), calls=%async_computation.20 | async-start | bytes 3604480 | tf_op jit(solution)/shard_map/all_gather | solution.py:69
  173.6 142.3 %all-gather.29.cloned.1.call-start = ((), (), s32[]{:S(2)}) async-start(), calls=%async_computation.21 | async-start | bytes 3604480 | tf_op jit(solution)/shard_map/all_gather | solution.py:70
  174.3 195.4 %all-gather.25.cloned.1.call-start = ((), (), s32[]{:S(2)}) async-start(), calls=%async_computation.19 | async-start | bytes 2359296 | tf_op jit(solution)/shard_map/all_gather | solution.py:124
  260.5 160.7 %all-gather.33.cloned.1.call-start = ((), (), s32[]{:S(2)}) async-start(), calls=%async_computation.24 | async-start | bytes 2359296 | tf_op jit(solution)/shard_map/all_gather | solution.py:61
  261.3 186.7 %all-gather.31.cloned.1.call-start = ((), (), s32[]{:S(2)}) async-start(), calls=%async_computation.22 | async-start | bytes 3604480 | tf_op jit(solution)/shard_map/all_gather | solution.py:71
  261.8 289.7 %reduce-scatter.17.cloned.1.call-start = ((), (), s32[]{:S(2)}) async-start(), calls=%async_computation.25 | async-start | bytes 4718592 | tf_op jit(solution)/shard_map/reduce_scatter | solution.py:145
  462.9 160.8 %all-gather.35.cloned.1.call-start = ((), (), s32[]{:S(2)}) async-start(), calls=%async_computation.26 | async-start | bytes 2359296 | tf_op jit(solution)/shard_map/all_gather | solution.py:153
  463.0 110.1 %copy-start.5 = (bf16[512,256]{1,0:T(8,128)(2,1)S(1)}, bf16[512,256]{1,0:T(8,128)(2,1)}, u32[]{:S(2)}) copy-start(bf16[512,256]{1,0:T(8,128)(2,1)} %param.13) | copy-start | bytes 786436
  575.2 142.6 %reduce-scatter.15.cloned.1.call-start = ((), (), s32[]{:S(2)}) async-start(), calls=%async_computation.23 | async-start | bytes 4718592 | tf_op jit(solution)/shard_map/reduce_scatter | solution.py:132
  581.2 225.0 %reduce-scatter.19.cloned.1.call-start = ((), (), s32[]{:S(2)}) async-start(), calls=%async_computation.27 | async-start | bytes 4718592 | tf_op jit(solution)/shard_map/reduce_scatter | solution.py:200
  658.4 5.8 copy-start.10
  673.8 190.1 %reduce-scatter.31.cloned.1.call-start = ((), (), s32[]{:S(2)}) async-start(), calls=%async_computation.33 | async-start | bytes 7208960 | tf_op jit(solution)/shard_map/reduce_scatter | solution.py:226
  695.2 226.7 %reduce-scatter.33.cloned.1.call-start = ((), (), s32[]{:S(2)}) async-start(), calls=%async_computation.34 | async-start | bytes 7208960 | tf_op jit(solution)/shard_map/reduce_scatter | solution.py:229
  695.8 284.1 %reduce-scatter.35.cloned.1.call-start = ((), (), s32[]{:S(2)}) async-start(), calls=%async_computation.35 | async-start | bytes 7208960 | tf_op jit(solution)/shard_map/reduce_scatter | solution.py:232
  702.2 312.3 %reduce-scatter.21.cloned.1.call-start = ((), (), s32[]{:S(2)}) async-start(), calls=%async_computation.28 | async-start | bytes 2621440 | tf_op jit(solution)/shard_map/reduce_scatter | solution.py:209
  709.4 339.6 %reduce-scatter.23.cloned.1.call-start = ((), (), s32[]{:S(2)}) async-start(), calls=%async_computation.29 | async-start | bytes 2621440 | tf_op jit(solution)/shard_map/reduce_scatter | solution.py:210
  710.1 373.6 %reduce-scatter.25.cloned.1.call-start = ((), (), s32[]{:S(2)}) async-start(), calls=%async_computation.30 | async-start | bytes 2621440 | tf_op jit(solution)/shard_map/reduce_scatter | solution.py:216
  710.9 407.4 %reduce-scatter.27.cloned.1.call-start = ((), (), s32[]{:S(2)}) async-start(), calls=%async_computation.31 | async-start | bytes 2621440 | tf_op jit(solution)/shard_map/reduce_scatter | solution.py:222
  711.6 441.3 %reduce-scatter.29.cloned.1.call-start = ((), (), s32[]{:S(2)}) async-start(), calls=%async_computation.32 | async-start | bytes 2621440 | tf_op jit(solution)/shard_map/reduce_scatter | solution.py:225
  717.8 110.0 %copy-start.3 = (f32[512,256]{1,0:T(8,128)S(1)}, f32[512,256]{1,0:T(8,128)}, u32[]{:S(2)}) copy-start(f32[512,256]{1,0:T(8,128)} %reduce-scatter.17.cloned.1.call-done) | copy-start | bytes 1572868
  717.8 110.0 %copy-start.6 = (bf16[512,256]{1,0:T(8,128)(2,1)S(1)}, bf16[512,256]{1,0:T(8,128)(2,1)}, u32[]{:S(2)}) copy-start(bf16[512,256]{1,0:T(8,128)(2,1)} %param.13) | copy-start | bytes 786436
  (21 other events, 33.4 us)
Sparse Core Ops, SparseCore 0:
  9.6 19.4 all-gather.14
  30.6 16.7 all-gather.16
  48.9 16.7 all-gather.18
  67.1 16.7 all-gather.20
  85.8 51.0 all-gather.12
  138.3 14.9 all-gather.22
  172.9 85.7 reduce-scatter.12
  260.3 26.8 all-gather.26
  288.8 27.0 all-gather.28
  318.6 51.0 all-gather.24
  371.9 49.2 all-gather.32
  422.7 25.2 all-gather.30
  463.0 88.4 reduce-scatter.16
  575.3 48.3 all-gather.34
  627.2 86.8 reduce-scatter.14
  718.0 88.2 reduce-scatter.18
  809.2 54.6 reduce-scatter.30
  867.0 54.8 reduce-scatter.32
  925.0 54.8 reduce-scatter.34
  983.0 31.4 reduce-scatter.20
  1017.6 31.3 reduce-scatter.22
  1052.3 31.4 reduce-scatter.24
  1086.9 31.4 reduce-scatter.26
  1121.4 31.4 reduce-scatter.28
where the time goes:
time: 1160 us
  waiting for transfers between devices  912 us (79%)
  matrix products  79.1 us (7%)
  blocking collectives  78.5 us (7%)
  local copies, waits for them, and re-layouts  44.2 us (4%)
  other arithmetic  29.5 us (3%)
  between operations  14.7 us (1%)
    reduce_scatter x1, waiting for transfers between devices, shards(): lax.psum_scatter(contract_cols(proj_grad, proj_weights), 'cols', scatter_...  86.5 us
    reduce_scatter x1, waiting for transfers between devices, shards(): lax.psum_scatter(contract_cols(pair_grad, pair_weights), 'cols', scatter_...  84.5 us
    reduce_scatter x1, waiting for transfers between devices, shards(): lax.psum_scatter(partial_attn, 'cols', scatter_dimension=1, tiled=True)  84.3 us
    reduce_scatter x1, waiting for transfers between devices, shards(): lax.psum_scatter(pair_weight_grad[:, hidden_local:], 'rows', scatter_dime...  58 us
    reduce_scatter x1, waiting for transfers between devices, shards(): lax.psum_scatter(down_grad, 'rows', scatter_dimension=1, tiled=True)  58 us
    all_gather x1, waiting for transfers between devices, shards(): lax.all_gather(tokens, 'cols', axis=1, tiled=True)  50.7 us
    all_gather x1, waiting for transfers between devices, shards(): lax.all_gather(middle.astype(jnp.bfloat16), 'cols', axis=1, tiled=True)  50 us
    all_gather x1, waiting for transfers between devices, shards(): lax.all_gather(middle_grad.astype(jnp.bfloat16), 'cols', axis=1, tiled=True)  42.4 us
  transfers between devices with their start and end apart: 24, of which 22 were waited for; matrix products, arithmetic and copies ran while one was open for 11% of the time, Pallas kernels for 0%

commit v1 on v0

--- a/solution.py
+++ b/solution.py
@@ -95,7 +95,10 @@
     queries = to_heads(jax.nn.silu(pre_query).astype(jnp.bfloat16))
     keys = to_heads(jax.nn.silu(pre_key).astype(jnp.bfloat16))
     values = to_heads(jax.nn.silu(pre_value).astype(jnp.bfloat16))
-    bounds = jnp.cumsum(lengths[0])
+    sequence_places = jnp.arange(lengths.shape[1], dtype=jnp.int32)
+    bounds = jnp.sum(
+        jnp.where(sequence_places[None, :] <= sequence_places[:, None], lengths[0][None, :], 0), axis=1
+    )
     places = jnp.arange(token_count, dtype=jnp.int32)
     member = jnp.sum((places[:, None] >= bounds[None, :]).astype(jnp.int32), axis=1)
     block_rows = min(512, token_count)

time: 1160 us -> 1160 us (level)
  no operation moved by 1% of the time
where the time goes in v1:
time: 1160 us
  waiting for transfers between devices  912 us (79%)
  matrix products  79.1 us (7%)
  blocking collectives  78.5 us (7%)
  local copies, waits for them, and re-layouts  44.2 us (4%)
  other arithmetic  29.5 us (3%)
  between operations  14.7 us (1%)
    reduce_scatter x1, waiting for transfers between devices, shards(): lax.psum_scatter(contract_cols(proj_grad, proj_weights), 'cols', scatter_...  86.5 us
    reduce_scatter x1, waiting for transfers between devices, shards(): lax.psum_scatter(contract_cols(pair_grad, pair_weights), 'cols', scatter_...  84.5 us
    reduce_scatter x1, waiting for transfers between devices, shards(): lax.psum_scatter(partial_attn, 'cols', scatter_dimension=1, tiled=True)  84.3 us
    reduce_scatter x1, waiting for transfers between devices, shards(): lax.psum_scatter(pair_weight_grad[:, hidden_local:], 'rows', scatter_dime...  58 us
    reduce_scatter x1, waiting for transfers between devices, shards(): lax.psum_scatter(down_grad, 'rows', scatter_dimension=1, tiled=True)  58 us
    all_gather x1, waiting for transfers between devices, shards(): lax.all_gather(tokens, 'cols', axis=1, tiled=True)  50.7 us
    all_gather x1, waiting for transfers between devices, shards(): lax.all_gather(middle.astype(jnp.bfloat16), 'cols', axis=1, tiled=True)  50 us
    all_gather x1, waiting for transfers between devices, shards(): lax.all_gather(middle_grad.astype(jnp.bfloat16), 'cols', axis=1, tiled=True)  42.4 us
  transfers between devices with their start and end apart: 24, of which 22 were waited for; matrix products, arithmetic and copies ran while one was open for 11% of the time, Pallas kernels for 0%

profile of v1, /device:TPU:0, one launch (start us, length us, event | category | flops | bytes accessed | tf_op | source)
XLA Modules:
  0.0 1159.7 jit_solution(1115558683745743242)
XLA Ops:
  12.9 16.2 %all-gather.15.cloned.1.call-done = bf16[2048,256]{1,0:T(8,128)(2,1)} async-done(((bf16[512,256]{1,0:T(8,128)(2,1)}), bf16[2048,256]{1,0:T(8,128)(2,1)}) %all-gather.15.cloned.1.call-update) | async-done | bytes 1048592 | tf_op jit(solution)/shard_map/all_gather | solution.py:64
  31.4 15.9 %all-gather.17.cloned.1.call-done = bf16[2048,256]{1,0:T(8,128)(2,1)} async-done(((bf16[512,256]{1,0:T(8,128)(2,1)}), bf16[2048,256]{1,0:T(8,128)(2,1)}) %all-gather.17.cloned.1.call-update) | async-done | bytes 1048592 | tf_op jit(solution)/shard_map/all_gather | solution.py:65
  49.7 16.0 %all-gather.19.cloned.1.call-done = bf16[2048,256]{1,0:T(8,128)(2,1)} async-done(((bf16[512,256]{1,0:T(8,128)(2,1)}), bf16[2048,256]{1,0:T(8,128)(2,1)}) %all-gather.19.cloned.1.call-update) | async-done | bytes 1048592 | tf_op jit(solution)/shard_map/all_gather | solution.py:66
  68.0 15.8 %all-gather.21.cloned.1.call-done = bf16[2048,256]{1,0:T(8,128)(2,1)} async-done(((bf16[512,256]{1,0:T(8,128)(2,1)}), bf16[2048,256]{1,0:T(8,128)(2,1)}) %all-gather.21.cloned.1.call-update) | async-done | bytes 1048592 | tf_op jit(solution)/shard_map/all_gather | solution.py:67
  86.2 50.7 %all-gather.13.cloned.1.call-done = bf16[512,2048]{1,0:T(8,128)(2,1)} async-done(((bf16[512,256]{1,0:T(8,128)(2,1)}), bf16[512,2048]{1,0:T(8,128)(2,1)}) %all-gather.13.cloned.1.call-update) | async-done | bytes 2097168 | tf_op jit(solution)/shard_map/all_gather | solution.py:60
  149.0 18.6 %psum.28 = f32[512]{0:T(512)S(1)} all-reduce(f32[512]{0:T(512)S(1)} %get-tuple-element.78), channel_id=1, replica_groups=mesh['rows'=4,'cols'=8] {'cols'}, use_global_device_ids=true, to_apply=%region_4.5 | all-reduce | flops 512 | bytes 4096 | tf_op jit(solution)/shard_map/psum | solution.py:119
  174.3 84.3 %reduce-scatter.13.cloned.1.call-done = f32[512,256]{1,0:T(8,128)} async-done(((f32[512,2048]{1,0:T(8,128)}), f32[512,256]{1,0:T(8,128)}) %reduce-scatter.13.cloned.1.call-update) | async-done | bytes 524304 | tf_op jit(solution)/shard_map/reduce_scatter | solution.py:125
  262.1 25.1 %all-gather.27.cloned.1.call-done = bf16[2048,704]{0,1:T(8,128)(2,1)} async-done(((bf16[512,704]{0,1:T(8,128)(2,1)}), bf16[2048,704]{0,1:T(8,128)(2,1)}) %all-gather.27.cloned.1.call-update) | async-done | bytes 2883600 | tf_op jit(solution)/shard_map/all_gather | solution.py:69
  290.9 25.0 %all-gather.29.cloned.1.call-done = bf16[2048,704]{0,1:T(8,128)(2,1)} async-done(((bf16[512,704]{0,1:T(8,128)(2,1)}), bf16[2048,704]{0,1:T(8,128)(2,1)}) %all-gather.29.cloned.1.call-update) | async-done | bytes 2883600 | tf_op jit(solution)/shard_map/all_gather | solution.py:70
  319.7 50.0 %all-gather.25.cloned.1.call-done = bf16[512,2048]{1,0:T(8,128)(2,1)} async-done(((bf16[512,256]{1,0:T(8,128)(2,1)}), bf16[512,2048]{1,0:T(8,128)(2,1)}) %all-gather.25.cloned.1.call-update) | async-done | bytes 2097168 | tf_op jit(solution)/shard_map/all_gather | solution.py:127
  371.9 7.8 fusion.4
  379.7 41.5 %all-gather.33.cloned.1.call-done = bf16[512,2048]{1,0:T(8,128)(2,1)} async-done(((bf16[512,256]{1,0:T(8,128)(2,1)}), bf16[512,2048]{1,0:T(8,128)(2,1)}) %all-gather.33.cloned.1.call-update) | async-done | bytes 2097168 | tf_op jit(solution)/shard_map/all_gather | solution.py:61
  421.2 26.8 %all-gather.31.cloned.1.call-done = bf16[704,2048]{1,0:T(8,128)(2,1)} async-done(((bf16[704,512]{1,0:T(8,128)(2,1)}), bf16[704,2048]{1,0:T(8,128)(2,1)}) %all-gather.31.cloned.1.call-update) | async-done | bytes 2883600 | tf_op jit(solution)/shard_map/all_gather | solution.py:71
  448.0 6.0 multiply_convert_fusion.3
  455.2 7.7 fusion.11
  467.0 84.5 %reduce-scatter.17.cloned.1.call-done = f32[512,256]{1,0:T(8,128)} async-done(((f32[512,2048]{1,0:T(8,128)}), f32[512,256]{1,0:T(8,128)}) %reduce-scatter.17.cloned.1.call-update) | async-done | bytes 524304 | tf_op jit(solution)/shard_map/reduce_scatter | solution.py:148
  552.9 20.2 %psum.29 = f32[512]{0:T(512)S(1)} all-reduce(f32[512]{0:T(512)S(1)} %multiply_reduce_fusion.2), channel_id=1, replica_groups=mesh['rows'=4,'cols'=8] {'cols'}, use_global_device_ids=true, to_apply=%region_10.11 | all-reduce | flops 512 | bytes 4096 | tf_op jit(solution)/shard_map/psum | solution.py:152
  581.2 42.4 %all-gather.35.cloned.1.call-done = bf16[512,2048]{1,0:T(8,128)(2,1)} async-done(((bf16[512,256]{1,0:T(8,128)(2,1)}), bf16[512,2048]{1,0:T(8,128)(2,1)}) %all-gather.35.cloned.1.call-update) | async-done | bytes 2097168 | tf_op jit(solution)/shard_map/all_gather | solution.py:156
  627.2 19.6 %psum.30 = f32[512]{0:T(512)S(1)} all-reduce(f32[512]{0:T(512)S(1)} %get-tuple-element.80), channel_id=1, replica_groups=mesh['rows'=4,'cols'=8] {'cols'}, use_global_device_ids=true, to_apply=%region_12.13 | all-reduce | flops 512 | bytes 4096 | tf_op jit(solution)/shard_map/psum | solution.py:161
  667.2 6.6 fusion.23
  674.9 9.6 fusion.2
  684.5 10.7 fusion.30
  719.7 86.5 %reduce-scatter.19.cloned.1.call-done = f32[512,256]{1,0:T(8,128)} async-done(((f32[512,2048]{1,0:T(8,128)}), f32[512,256]{1,0:T(8,128)}) %reduce-scatter.19.cloned.1.call-update) | async-done | bytes 524304 | tf_op jit(solution)/shard_map/reduce_scatter | solution.py:203
  807.6 20.2 %psum.31 = f32[512]{0:T(512)S(1)} all-reduce(f32[512]{0:T(512)S(1)} %multiply_reduce_fusion), channel_id=1, replica_groups=mesh['rows'=4,'cols'=8] {'cols'}, use_global_device_ids=true, to_apply=%region_15.16 | all-reduce | flops 512 | bytes 4096 | tf_op jit(solution)/shard_map/psum | solution.py:207
  830.3 33.6 %reduce-scatter.31.cloned.1.call-done = f32[512,704]{0,1:T(8,128)} async-done(((f32[2048,704]{0,1:T(8,128)}), f32[512,704]{0,1:T(8,128)}) %reduce-scatter.31.cloned.1.call-update) | async-done | bytes 1441808 | tf_op jit(solution)/shard_map/reduce_scatter | solution.py:229
  863.8 58.0 %reduce-scatter.33.cloned.1.call-done = f32[512,704]{0,1:T(8,128)} async-done(((f32[2048,704]{0,1:T(8,128)}), f32[512,704]{0,1:T(8,128)}) %reduce-scatter.33.cloned.1.call-update) | async-done | bytes 1441808 | tf_op jit(solution)/shard_map/reduce_scatter | solution.py:232
  921.9 58.0 %reduce-scatter.35.cloned.1.call-done = f32[704,512]{1,0:T(8,128)} async-done(((f32[704,2048]{1,0:T(8,128)}), f32[704,512]{1,0:T(8,128)}) %reduce-scatter.35.cloned.1.call-update) | async-done | bytes 1441808 | tf_op jit(solution)/shard_map/reduce_scatter | solution.py:235
  979.9 34.6 %reduce-scatter.21.cloned.1.call-done = f32[512,256]{1,0:T(8,128)} async-done(((f32[2048,256]{1,0:T(8,128)}), f32[512,256]{1,0:T(8,128)}) %reduce-scatter.21.cloned.1.call-update) | async-done | bytes 524304 | tf_op jit(solution)/shard_map/reduce_scatter | solution.py:212
  1014.5 34.5 %reduce-scatter.23.cloned.1.call-done = f32[512,256]{1,0:T(8,128)} async-done(((f32[2048,256]{1,0:T(8,128)}), f32[512,256]{1,0:T(8,128)}) %reduce-scatter.23.cloned.1.call-update) | async-done | bytes 524304 | tf_op jit(solution)/shard_map/reduce_scatter | solution.py:213
  1049.0 34.8 %reduce-scatter.25.cloned.1.call-done = f32[512,256]{1,0:T(8,128)} async-done(((f32[2048,256]{1,0:T(8,128)}), f32[512,256]{1,0:T(8,128)}) %reduce-scatter.25.cloned.1.call-update) | async-done | bytes 524304 | tf_op jit(solution)/shard_map/reduce_scatter | solution.py:219
  1083.8 34.6 %reduce-scatter.27.cloned.1.call-done = f32[512,256]{1,0:T(8,128)} async-done(((f32[2048,256]{1,0:T(8,128)}), f32[512,256]{1,0:T(8,128)}) %reduce-scatter.27.cloned.1.call-update) | async-done | bytes 524304 | tf_op jit(solution)/shard_map/reduce_scatter | solution.py:225
  1118.3 34.6 %reduce-scatter.29.cloned.1.call-done = f32[256,512]{1,0:T(8,128)} async-done(((f32[256,2048]{1,0:T(8,128)}), f32[256,512]{1,0:T(8,128)}) %reduce-scatter.29.cloned.1.call-update) | async-done | bytes 524304 | tf_op jit(solution)/shard_map/reduce_scatter | solution.py:228
  (160 shorter events, 114.8 us)
Async XLA Ops:
  7.2 5.2 copy-start.24
  7.2 5.2 copy-start.25
  7.2 21.9 %all-gather.15.cloned.1.call-start = ((), (), s32[]{:S(2)}) async-start(), calls=%async_computation.13 | async-start | bytes 1310720 | tf_op jit(solution)/shard_map/all_gather | solution.py:64
  7.9 39.4 %all-gather.17.cloned.1.call-start = ((), (), s32[]{:S(2)}) async-start(), calls=%async_computation.14 | async-start | bytes 1310720 | tf_op jit(solution)/shard_map/all_gather | solution.py:65
  8.7 57.0 %all-gather.19.cloned.1.call-start = ((), (), s32[]{:S(2)}) async-start(), calls=%async_computation.15 | async-start | bytes 1310720 | tf_op jit(solution)/shard_map/all_gather | solution.py:66
  9.4 74.5 %all-gather.21.cloned.1.call-start = ((), (), s32[]{:S(2)}) async-start(), calls=%async_computation.16 | async-start | bytes 1310720 | tf_op jit(solution)/shard_map/all_gather | solution.py:67
  10.0 126.9 %all-gather.13.cloned.1.call-start = ((), (), s32[]{:S(2)}) async-start(), calls=%async_computation.12 | async-start | bytes 2359296 | tf_op jit(solution)/shard_map/all_gather | solution.py:60
  10.6 158.3 %all-gather.23.cloned.1.call-start = ((), (), s32[]{:S(2)}) async-start(), calls=%async_computation.17 | async-start | bytes 1310720 | tf_op jit(solution)/shard_map/all_gather | solution.py:68
  11.2 247.5 %reduce-scatter.13.cloned.1.call-start = ((), (), s32[]{:S(2)}) async-start(), calls=%async_computation.18 | async-start | bytes 4718592 | tf_op jit(solution)/shard_map/reduce_scatter | solution.py:125
  12.9 132.9 %copy-start.15 = (pred[512,512]{1,0:T(8,128)(4,1)}, pred[512,512]{1,0:T(8,128)(4,1)S(1)}, u32[]{:S(2)}) copy-start(pred[512,512]{1,0:T(8,128)(4,1)S(1)} %fusion.10) | copy-start | bytes 786436
  172.8 85.9 %copy-start.7 = (bf16[512,256]{1,0:T(8,128)(2,1)S(1)}, bf16[512,256]{1,0:T(8,128)(2,1)}, u32[]{:S(2)}) copy-start(bf16[512,256]{1,0:T(8,128)(2,1)} %param.12) | copy-start | bytes 786436
  172.8 114.4 %all-gather.27.cloned.1.call-start = ((), (), s32[]{:S(2)}) async-start(), calls=%async_computation.20 | async-start | bytes 3604480 | tf_op jit(solution)/shard_map/all_gather | solution.py:69
  173.6 142.3 %all-gather.29.cloned.1.call-start = ((), (), s32[]{:S(2)}) async-start(), calls=%async_computation.21 | async-start | bytes 3604480 | tf_op jit(solution)/shard_map/all_gather | solution.py:70
  174.3 195.4 %all-gather.25.cloned.1.call-start = ((), (), s32[]{:S(2)}) async-start(), calls=%async_computation.19 | async-start | bytes 2359296 | tf_op jit(solution)/shard_map/all_gather | solution.py:127
  260.5 160.7 %all-gather.33.cloned.1.call-start = ((), (), s32[]{:S(2)}) async-start(), calls=%async_computation.24 | async-start | bytes 2359296 | tf_op jit(solution)/shard_map/all_gather | solution.py:61
  261.3 186.7 %all-gather.31.cloned.1.call-start = ((), (), s32[]{:S(2)}) async-start(), calls=%async_computation.22 | async-start | bytes 3604480 | tf_op jit(solution)/shard_map/all_gather | solution.py:71
  261.8 289.7 %reduce-scatter.17.cloned.1.call-start = ((), (), s32[]{:S(2)}) async-start(), calls=%async_computation.25 | async-start | bytes 4718592 | tf_op jit(solution)/shard_map/reduce_scatter | solution.py:148
  462.9 160.8 %all-gather.35.cloned.1.call-start = ((), (), s32[]{:S(2)}) async-start(), calls=%async_computation.26 | async-start | bytes 2359296 | tf_op jit(solution)/shard_map/all_gather | solution.py:156
  463.0 110.1 %copy-start.5 = (bf16[512,256]{1,0:T(8,128)(2,1)S(1)}, bf16[512,256]{1,0:T(8,128)(2,1)}, u32[]{:S(2)}) copy-start(bf16[512,256]{1,0:T(8,128)(2,1)} %param.13) | copy-start | bytes 786436
  575.2 142.6 %reduce-scatter.15.cloned.1.call-start = ((), (), s32[]{:S(2)}) async-start(), calls=%async_computation.23 | async-start | bytes 4718592 | tf_op jit(solution)/shard_map/reduce_scatter | solution.py:135
  581.2 225.0 %reduce-scatter.19.cloned.1.call-start = ((), (), s32[]{:S(2)}) async-start(), calls=%async_computation.27 | async-start | bytes 4718592 | tf_op jit(solution)/shard_map/reduce_scatter | solution.py:203
  658.4 5.8 copy-start.10
  673.8 190.1 %reduce-scatter.31.cloned.1.call-start = ((), (), s32[]{:S(2)}) async-start(), calls=%async_computation.33 | async-start | bytes 7208960 | tf_op jit(solution)/shard_map/reduce_scatter | solution.py:229
  695.2 226.7 %reduce-scatter.33.cloned.1.call-start = ((), (), s32[]{:S(2)}) async-start(), calls=%async_computation.34 | async-start | bytes 7208960 | tf_op jit(solution)/shard_map/reduce_scatter | solution.py:232
  695.8 284.1 %reduce-scatter.35.cloned.1.call-start = ((), (), s32[]{:S(2)}) async-start(), calls=%async_computation.35 | async-start | bytes 7208960 | tf_op jit(solution)/shard_map/reduce_scatter | solution.py:235
  702.2 312.3 %reduce-scatter.21.cloned.1.call-start = ((), (), s32[]{:S(2)}) async-start(), calls=%async_computation.28 | async-start | bytes 2621440 | tf_op jit(solution)/shard_map/reduce_scatter | solution.py:212
  709.4 339.6 %reduce-scatter.23.cloned.1.call-start = ((), (), s32[]{:S(2)}) async-start(), calls=%async_computation.29 | async-start | bytes 2621440 | tf_op jit(solution)/shard_map/reduce_scatter | solution.py:213
  710.1 373.6 %reduce-scatter.25.cloned.1.call-start = ((), (), s32[]{:S(2)}) async-start(), calls=%async_computation.30 | async-start | bytes 2621440 | tf_op jit(solution)/shard_map/reduce_scatter | solution.py:219
  710.9 407.4 %reduce-scatter.27.cloned.1.call-start = ((), (), s32[]{:S(2)}) async-start(), calls=%async_computation.31 | async-start | bytes 2621440 | tf_op jit(solution)/shard_map/reduce_scatter | solution.py:225
  711.6 441.3 %reduce-scatter.29.cloned.1.call-start = ((), (), s32[]{:S(2)}) async-start(), calls=%async_computation.32 | async-start | bytes 2621440 | tf_op jit(solution)/shard_map/reduce_scatter | solution.py:228
  717.8 110.0 %copy-start.3 = (f32[512,256]{1,0:T(8,128)S(1)}, f32[512,256]{1,0:T(8,128)}, u32[]{:S(2)}) copy-start(f32[512,256]{1,0:T(8,128)} %reduce-scatter.17.cloned.1.call-done) | copy-start | bytes 1572868
  717.8 110.0 %copy-start.6 = (bf16[512,256]{1,0:T(8,128)(2,1)S(1)}, bf16[512,256]{1,0:T(8,128)(2,1)}, u32[]{:S(2)}) copy-start(bf16[512,256]{1,0:T(8,128)(2,1)} %param.13) | copy-start | bytes 786436
  (21 other events, 33.4 us)
Sparse Core Ops, SparseCore 0:
  9.6 19.4 all-gather.14
  30.6 16.7 all-gather.16
  48.9 16.7 all-gather.18
  67.1 16.7 all-gather.20
  85.8 51.0 all-gather.12
  138.3 14.9 all-gather.22
  172.9 85.7 reduce-scatter.12
  260.3 26.8 all-gather.26
  288.8 27.0 all-gather.28
  318.6 51.0 all-gather.24
  371.9 49.2 all-gather.32
  422.7 25.2 all-gather.30
  463.0 88.4 reduce-scatter.16
  575.3 48.3 all-gather.34
  627.2 86.8 reduce-scatter.14
  718.0 88.2 reduce-scatter.18
  809.2 54.6 reduce-scatter.30
  867.0 54.8 reduce-scatter.32
  925.0 54.8 reduce-scatter.34
  983.0 31.4 reduce-scatter.20
  1017.6 31.3 reduce-scatter.22
  1052.3 31.4 reduce-scatter.24
  1086.9 31.4 reduce-scatter.26
  1121.4 31.4 reduce-scatter.28
